TPU v7x, 32 devices: a whole 2x2x4 slice. The times are simulated.
32 devices in a mesh: parts: 2 (over y), rep: 4 (over x, core), tp: 4 (over z).
Axes of the slice: x: 2, y: 2, z: 4, core: 2. Of those that a mesh axis runs over, the one named last changes fastest.
Arguments:
- tokens: bfloat16 [2048, 8192], P(('parts', 'rep'), 'tp'), parts along dimension 0, may hold values from -6 to 6
- base_output_weight: bfloat16 [8192, 8192], P('tp', 'rep'), may hold values from -0.0625 to 0.0625
- token_adapter_index: int32 [2048], P('parts'), parts along dimension 0, may hold values from 0 to 7
- adapter_rank_block_count: int32 [8], replicated, may hold values from 1 to 8
- adapter_input_factors: bfloat16 [8, 8192, 128], P('rep', 'tp'), may hold values from -0.0625 to 0.0625
- adapter_output_factors: bfloat16 [8, 128, 8192], P('tp', None, 'rep'), may hold values from -0.5 to 0.5
Outputs:
- mixed: bfloat16 [2048, 8192], P(('parts', 'tp'), 'rep'), parts along dimension 0
There are 2 independent parts, one for each index of `parts`. A program takes and returns all parts, laid end to end along the dimension named above; an argument that names none is the same for every part. Nothing has to cross between parts.
All inputs are finite; a program needn't handle non-finite values.
Results may differ from a plain program's by a relative error of at most 0.009.
Values may be sent and summed in bfloat16 or wider, within the bound.
A program may use at most 64 MiB of HBM per device.

v0:
```python
import jax
import jax.numpy as jnp
from jax import lax
from jax.sharding import PartitionSpec as P

RBLK = 16


def body(
    tokens,
    base_output_weight,
    token_adapter_index,
    adapter_rank_block_count,
    adapter_input_factors,
    adapter_output_factors,
):
    rep_index = lax.axis_index("rep")
    tp_index = lax.axis_index("tp")
    collected_factors = lax.all_gather(tokens, "rep", axis=0, tiled=True)
    replica_share = adapter_input_factors.shape[0]
    tensor_parallel_share = adapter_output_factors.shape[0]
    table = token_adapter_index[:, None] == jnp.arange(adapter_rank_block_count.shape[0])[None, :]
    rank = RBLK * jnp.sum(jnp.where(table, adapter_rank_block_count[None, :], 0), axis=1)
    owned_in = (
        token_adapter_index[:, None] - rep_index * replica_share
        == jnp.arange(replica_share)[None, :]
    )
    projected_rows = jnp.einsum(
        "ho,nof->hnf", collected_factors, adapter_input_factors, preferred_element_type=jnp.float32
    )
    partial_value = jnp.sum(jnp.where(owned_in[:, :, None], projected_rows, 0.0), axis=1)
    lowrank = lax.psum(partial_value, ("rep", "tp"))
    keep = jnp.arange(lowrank.shape[1])[None, :] < rank[:, None]
    scale = 8.0 / jnp.sqrt(rank.astype(jnp.float32))
    scaled = jnp.where(keep, lowrank * scale[:, None], 0.0).astype(jnp.bfloat16)
    owned_out = (
        token_adapter_index[:, None] - tp_index * tensor_parallel_share
        == jnp.arange(tensor_parallel_share)[None, :]
    )
    spread_rows = jnp.where(owned_out[:, :, None], scaled[:, None, :], jnp.zeros((), jnp.bfloat16))
    base_part = jnp.dot(collected_factors, base_output_weight, preferred_element_type=jnp.float32)
    return lax.psum_scatter(
        (
            base_part
            + jnp.einsum(
                "zpe,peg->zg",
                spread_rows,
                adapter_output_factors,
                preferred_element_type=jnp.float32,
            )
        ).astype(jnp.bfloat16),
        "tp",
        scatter_dimension=0,
        tiled=True,
    )


def solution(mesh):
    placed = (
        P(("parts", "rep"), "tp"),
        P("tp", "rep"),
        P("parts"),
        P(),
        P("rep", "tp", None),
        P("tp", None, "rep"),
    )
    return jax.shard_map(
        body, mesh=mesh, in_specs=placed, out_specs=P(("parts", "tp"), "rep"), check_vma=False
    )
```

profile of v0, /device:TPU:0, one launch (start us, length us, event | category | flops | bytes accessed | tf_op | source)
XLA Modules:
  0.0 231.9 jit_solution(5546250777389410467)
XLA Ops:
  6.5 0.0 copy-start
  6.5 0.0 all-gather.2.cloned.1.call-start
  6.5 0.7 all-gather.2.cloned.1.call-update
  7.3 0.0 all-reduce.2.cloned.1.call-start
  7.3 0.8 select_reduce_fusion
  8.1 0.7 broadcast_subtract_fusion
  8.8 37.3 %all-gather.2.cloned.1.call-done = bf16[1024,2048]{1,0:T(8,128)(2,1)} async-done(((bf16[256,2048]{1,0:T(8,128)(2,1)}), bf16[1024,2048]{1,0:T(8,128)(2,1)}) %all-gather.2.cloned.1.call-update) | async-done | bytes 4194320 | tf_op jit(solution)/shard_map/all_gather | solution.py:19
  46.1 4.6 %fusion.6 = f32[1024,128]{1,0:T(8,128)} fusion(bf16[2,2048,128]{2,1,0:T(8,128)(2,1)} %param.10, bf16[1024,2048]{1,0:T(8,128)(2,1)} %all-gather.2.cloned.1.call-done, pred[1024,2]{0,1:T(4,128)(4,1)S(1)} %iota_compare_fusion.2), kind=kOutput, calls=%fused_computation.5 | convolution fusion | flops 1074135040 | bytes 5769216 | tf_op jit(solution)/shard_map/ho,nof->hnf/dot_general | solution.py:28
  50.7 0.0 all-reduce.2.cloned.1.call-update
  50.7 0.0 reduce-scatter.2.cloned.1.call-start
  50.8 14.4 %fusion.14 = f32[1024,2048]{1,0:T(8,128)} fusion(bf16[1024,2048]{1,0:T(8,128)(2,1)} %all-gather.2.cloned.1.call-done, bf16[2048,2048]{1,0:T(8,128)(2,1)} %param.7), kind=kOutput, calls=%fused_computation.21 | convolution fusion | flops 8589934592 | bytes 20971520 | tf_op jit(solution)/shard_map/dot_general | solution.py:41
  65.2 75.8 %all-reduce.2.cloned.1.call-done = f32[1024,128]{1,0:T(8,128)} async-done(((f32[1024,128]{1,0:T(8,128)}), f32[1024,128]{1,0:T(8,128)}) %all-reduce.2.cloned.1.call-update) | async-done | bytes 524304 | tf_op jit(solution)/shard_map/psum | solution.py:32
  141.0 1.4 select_convert_fusion
  142.4 0.0 copy-done
  142.4 5.5 %fusion = bf16[1024,2048]{1,0:T(8,128)(2,1)} fusion(f32[1024,2048]{1,0:T(8,128)} %fusion.14, bf16[2,128,2048]{2,1,0:T(8,128)(2,1)S(1)} %copy-done, pred[1024,2]{0,1:T(4,128)(4,1)S(1)} %iota_compare_fusion.3, bf16[1024,128]{1,0:T(8,128)(2,1)S(1)} %select_convert_fusion), kind=kOutput, calls=%fused_computation.1 | convolution fusion | flops 1078198272 | bytes 13895680 | tf_op jit(solution)/shard_map/zpe,peg->zg/dot_general | solution.py:45
  147.9 0.0 reduce-scatter.2.cloned.1.call-update
  148.0 77.4 %reduce-scatter.2.cloned.1.call-done = bf16[256,2048]{1,0:T(8,128)(2,1)} async-done(((bf16[1024,2048]{1,0:T(8,128)(2,1)}), bf16[256,2048]{1,0:T(8,128)(2,1)}) %reduce-scatter.2.cloned.1.call-update) | async-done | bytes 1048592 | tf_op jit(solution)/shard_map/reduce_scatter | solution.py:42
  (4 shorter events, 0.0 us)
Async XLA Ops:
  6.5 135.8 %copy-start = (bf16[2,128,2048]{2,1,0:T(8,128)(2,1)S(1)}, bf16[2,128,2048]{2,1,0:T(8,128)(2,1)}, u32[]{:S(2)}) copy-start(bf16[2,128,2048]{2,1,0:T(8,128)(2,1)} %param.11) | copy-start | bytes 3145732
  6.5 39.6 %all-gather.2.cloned.1.call-start = ((), (), s32[]{:S(2)}) async-start(), calls=%async_computation.1 | async-start | bytes 5242880 | tf_op jit(solution)/shard_map/all_gather | solution.py:19
  7.3 133.7 %all-reduce.2.cloned.1.call-start = ((), (), s32[]{:S(2)}) async-start(), calls=%async_computation.2 | async-start | bytes 1048576 | tf_op jit(solution)/shard_map/psum | solution.py:32
  50.7 174.7 %reduce-scatter.2.cloned.1.call-start = ((), (), s32[]{:S(2)}) async-start(), calls=%async_computation.3 | async-start | bytes 5242880 | tf_op jit(solution)/shard_map/reduce_scatter | solution.py:42
Sparse Core Ops, SparseCore 0:
  8.9 37.1 all-gather.1
  50.8 90.1 all-reduce.1
  148.1 77.2 reduce-scatter.1
where the time goes:
time: 232 us
  waiting for transfers between devices  191 us (82%)
  matrix products  24.5 us (11%)
  between operations  13.2 us (6%)
  other arithmetic  2.89 us (1%)
    reduce_scatter x1, waiting for transfers between devices, body(): lax.psum_scatter((base_part + jnp.einsum('zpe,peg->zg', spread_rows, adap...  77.4 us
    psum x1, waiting for transfers between devices, body(): lowrank = lax.psum(partial_value, ('rep', 'tp'))  75.8 us
    all_gather x1, waiting for transfers between devices, body(): collected_factors = lax.all_gather(tokens, 'rep', axis=0, tiled=True)  37.3 us
    dot_general x1, matrix products, body(): jnp.dot(collected_factors, base_output_weight, preferred_element_type=jnp...  14.4 us
    dot_general x1, matrix products, body(): jnp.einsum('zpe,peg->zg', spread_rows, adapter_output_factors, preferred_...  5.55 us
  transfers between devices with their start and end apart: 3, of which 3 were waited for; matrix products, arithmetic and copies ran while one was open for 7% of the time, Pallas kernels for 0%

commit v1 on v0

v1 whole, which is shorter than its diff:
```python
import functools

import jax
import jax.numpy as jnp
from jax import lax
from jax.experimental import pallas as pl
from jax.experimental.pallas import tpu as pltpu
from jax.sharding import PartitionSpec as P

RBLK = 16
STEPS = 4
MESH = pl.DeviceIdType.MESH


def kernel(
    reps,
    tps,
    steps,
    tokens,
    weight,
    factors_in,
    factors_out,
    adapter,
    scale,
    out,
    tok,
    w,
    fin,
    fout,
    base,
    acc,
    up,
    down,
    done,
    ask,
    asked,
    low,
    lows,
    spread,
    load_sem,
    own_sem,
    out_sem,
    tok_send,
    tok_fwd,
    tok_recv,
    a_send,
    a_recv,
    b_send,
    b_recv,
    c_send,
    c_recv,
    up_send,
    up_recv,
    down_send,
    down_recv,
):
    r = lax.axis_index("rep")
    t = lax.axis_index("tp")
    rows = tokens.shape[0]
    q = rows // steps
    width = weight.shape[1]
    tile = min(width, 512)
    in_share, out_share = fin.shape[0], fout.shape[0]
    rank = fin.shape[2]
    f32, bf16 = jnp.float32, jnp.bfloat16
    sibling = r + 1 - 2 * (r % 2)
    peers = [(r + 2 * j) % reps for j in range(1, reps // 2)]

    def remote(src, dst, send, recv, **where):
        return pltpu.make_async_remote_copy(
            src_ref=src, dst_ref=dst, send_sem=send, recv_sem=recv, device_id=where, device_id_type=MESH
        )

    loads = [
        pltpu.make_async_copy(src, dst, load_sem.at[i])
        for i, (src, dst) in enumerate(((factors_in, fin), (weight, w), (factors_out, fout)))
    ]
    for copy in loads:
        copy.start()

    def own(s):
        return pltpu.make_async_copy(tokens.at[pl.ds(s * q, q)], tok.at[s, r], own_sem.at[s])

    for s in range(steps):
        own(s).start()

    barrier = pltpu.get_barrier_semaphore()
    for j in range(1, reps):
        pl.semaphore_signal(barrier, inc=1, device_id={"rep": (r + j) % reps}, device_id_type=MESH)
    for j in range(1, tps):
        pl.semaphore_signal(barrier, inc=1, device_id={"tp": (t + j) % tps}, device_id_type=MESH)
    pl.semaphore_wait(barrier, reps + tps - 2)

    def token_copy(s, block, to, send, from_tokens):
        src = tokens.at[pl.ds(s * q, q)] if from_tokens else tok.at[s, block]
        return remote(src, tok.at[s, block], send, tok_recv.at[s, block], rep=to)

    def gather_start(s):
        for j, peer in enumerate(peers):
            token_copy(s, r, peer, tok_send.at[s, j], True).start()
        token_copy(s, r, sibling, tok_send.at[s, len(peers)], True).start()

    def gather_finish(s):
        own(s).wait()
        for j, peer in enumerate(peers):
            token_copy(s, peer, peer, tok_send.at[s, j], False).wait_recv()
            token_copy(s, peer, sibling, tok_fwd.at[s, j], False).start()
        token_copy(s, sibling, sibling, tok_send.at[s, len(peers)], False).wait_recv()
        for peer in peers:
            other = peer + 1 - 2 * (peer % 2)
            token_copy(s, other, sibling, tok_send.at[s, 0], False).wait_recv()

    def lowrank_ask(s):
        rowsall = tok[s].reshape(reps * q, tok.shape[3])
        chosen = jnp.zeros((reps * q, rank), f32)
        wanted = adapter[s].reshape(reps * q, rank) - r * in_share
        for n in range(in_share):
            product = jnp.dot(rowsall, fin[n], preferred_element_type=f32)
            chosen = jnp.where(wanted == n, product, chosen)
        ask[s] = chosen.astype(bf16).reshape(reps, q, rank)
        for j in range(1, reps):
            a_copy(s, (r + j) % reps, r, j).start()

    def a_copy(s, to, slot, j):
        return remote(ask.at[s, to], asked.at[s, slot], a_send.at[s, j], a_recv.at[s, slot], rep=to)

    def lowrank_sum(s):
        total = ask[s, r].astype(f32)
        for j in range(1, reps):
            peer = (r + j) % reps
            a_copy(s, peer, peer, j).wait_recv()
            total += asked[s, peer].astype(f32)
        lows[s, t] = total.astype(bf16)
        for j in range(1, tps):
            b_copy(s, (t + j) % tps, t, j).start()

    def b_copy(s, to, slot, j):
        return remote(lows.at[s, slot], lows.at[s, slot], b_send.at[s, j], b_recv.at[s, slot], tp=to)

    def lowrank_scale(s):
        for j in range(1, tps):
            peer = (t + j) % tps
            b_copy(s, peer, peer, j).wait_recv()
        total = lows[s, 0].astype(f32)
        for k in range(1, tps):
            total += lows[s, k].astype(f32)
        low[s, r] = (total * scale[s, r]).astype(bf16)
        for j in range(1, reps):
            c_copy(s, (r + j) % reps, r, j).start()

    def c_copy(s, to, slot, j):
        return remote(low.at[s, slot], low.at[s, slot], c_send.at[s, j], c_recv.at[s, slot], rep=to)

    def lowrank_wait(s):
        for j in range(1, reps):
            peer = (r + j) % reps
            c_copy(s, peer, peer, j).wait_recv()

    def project(s):
        @pl.loop(0, width // tile)
        def _(i):
            columns = pl.ds(pl.multiple_of(i * tile, tile), tile)
            base[:, columns] = jnp.dot(
                tok[s].reshape(reps * q, tok.shape[3]), w[:, columns], preferred_element_type=f32
            )

    def adapt(s):
        mine = adapter[s].reshape(reps * q, rank) - t * out_share
        value = low[s].reshape(reps * q, rank)
        for n in range(out_share):
            spread[:, n * rank : (n + 1) * rank] = jnp.where(
                mine == n, value.astype(f32), 0.0
            ).astype(bf16)

        @pl.loop(0, width // tile)
        def _(i):
            columns = pl.ds(pl.multiple_of(i * tile, tile), tile)
            block = fout[:, :, columns].reshape(out_share * rank, tile)
            delta = jnp.dot(spread[...], block, preferred_element_type=f32)
            acc[s, :, :, columns] = (base[:, columns] + delta).astype(bf16).reshape(tps, q, tile)

    def up_copy(s, src, b, to):
        return remote(src.at[s, b], up.at[s, b], up_send.at[s, b], up_recv.at[s, b], tp=to)

    def down_copy(s, src, b, to):
        return remote(src.at[s, b], down.at[s, b], down_send.at[s, b], down_recv.at[s, b], tp=to)

    above = jnp.minimum(t + 1, tps - 1)
    below = jnp.maximum(t - 1, 0)

    def ends_send(s):
        @pl.when(t == 0)
        def _():
            for b in range(tps - 1, 0, -1):
                up_copy(s, acc, b, 1).start()

        @pl.when(t == tps - 1)
        def _():
            for b in range(tps - 1):
                down_copy(s, acc, b, tps - 2).start()

    def write(s):
        return pltpu.make_async_copy(done.at[s], out.at[pl.ds(s * q, q)], out_sem.at[s])

    def pass_on(s):
        for j in range(tps):
            b = tps - 1 - j

            @pl.when((t > 0) & (b > t))
            def _():
                up_copy(s, up, b, t - 1).wait_recv()
                up[s, b] = (up[s, b].astype(f32) + acc[s, b].astype(f32)).astype(bf16)
                up_copy(s, up, b, t + 1).start()

            @pl.when((t < tps - 1) & (j < t))
            def _():
                down_copy(s, down, j, t + 1).wait_recv()
                down[s, j] = (down[s, j].astype(f32) + acc[s, j].astype(f32)).astype(bf16)
                down_copy(s, down, j, t - 1).start()

        @pl.when(t == 0)
        def _():
            down_copy(s, down, 0, 1).wait_recv()
            done[s] = (acc[s, 0].astype(f32) + down[s, 0].astype(f32)).astype(bf16)

        @pl.when(t == tps - 1)
        def _():
            up_copy(s, up, tps - 1, tps - 2).wait_recv()
            done[s] = (acc[s, tps - 1].astype(f32) + up[s, tps - 1].astype(f32)).astype(bf16)

        @pl.when((t > 0) & (t < tps - 1))
        def _():
            up_copy(s, up, t, t - 1).wait_recv()
            down_copy(s, down, t, t + 1).wait_recv()
            done[s] = (
                acc[s, t].astype(f32) + up[s, t].astype(f32) + down[s, t].astype(f32)
            ).astype(bf16)

        write(s).start()

    gather_start(0)
    loads[0].wait()
    gather_finish(0)
    if steps > 1:
        gather_start(1)
    lowrank_ask(0)
    loads[1].wait()
    project(0)
    lowrank_sum(0)
    lowrank_scale(0)
    loads[2].wait()
    for s in range(steps):
        more = s + 1 < steps
        if more:
            gather_finish(s + 1)
            if s + 2 < steps:
                gather_start(s + 2)
            lowrank_ask(s + 1)
        lowrank_wait(s)
        adapt(s)
        if more:
            lowrank_sum(s + 1)
        ends_send(s)
        if more:
            project(s + 1)
            lowrank_scale(s + 1)
        if s > 0:
            pass_on(s - 1)
    pass_on(steps - 1)

    for s in range(steps):
        for j, peer in enumerate(peers):
            token_copy(s, r, peer, tok_send.at[s, j], True).wait_send()
            token_copy(s, peer, sibling, tok_fwd.at[s, j], False).wait_send()
        token_copy(s, r, sibling, tok_send.at[s, len(peers)], True).wait_send()
        for j in range(1, reps):
            a_copy(s, (r + j) % reps, r, j).wait_send()
            c_copy(s, (r + j) % reps, r, j).wait_send()
        for j in range(1, tps):
            b_copy(s, (t + j) % tps, t, j).wait_send()
        for b in range(tps):

            @pl.when(b > t)
            def _():
                up_copy(s, up, b, t + 1).wait_send()

            @pl.when(b < t)
            def _():
                down_copy(s, down, b, t - 1).wait_send()

        write(s).wait()


def body(reps, tps, tokens, weight, token_adapter_index, block_count, factors_in, factors_out):
    rows, depth = tokens.shape
    width = weight.shape[1]
    in_share, _, rank = factors_in.shape
    out_share = factors_out.shape[0]
    steps = STEPS
    q = rows // steps
    table = token_adapter_index[:, None] == jnp.arange(block_count.shape[0])[None, :]
    ranks = RBLK * jnp.sum(jnp.where(table, block_count[None, :], 0), axis=1)
    keep = jnp.arange(rank)[None, :] < ranks[:, None]
    scale = jnp.where(keep, (8.0 / jnp.sqrt(ranks.astype(jnp.float32)))[:, None], 0.0)
    adapter = jnp.broadcast_to(token_adapter_index[:, None], scale.shape)

    def by_step(x):
        return x.reshape(reps, steps, q, rank).transpose(1, 0, 2, 3)

    vmem = pl.BlockSpec(memory_space=pltpu.VMEM)
    hbm = pl.BlockSpec(memory_space=pl.ANY)
    f32, bf16 = jnp.float32, jnp.bfloat16
    dma = pltpu.SemaphoreType.DMA
    return pl.pallas_call(
        functools.partial(kernel, reps, tps, steps),
        out_shape=jax.ShapeDtypeStruct((rows, width), bf16),
        in_specs=[hbm, hbm, hbm, hbm, vmem, vmem],
        out_specs=hbm,
        scratch_shapes=[
            pltpu.VMEM((steps, reps, q, depth), bf16),
            pltpu.VMEM(weight.shape, bf16),
            pltpu.VMEM(factors_in.shape, bf16),
            pltpu.VMEM(factors_out.shape, bf16),
            pltpu.VMEM((reps * q, width), f32),
            pltpu.VMEM((steps, tps, q, width), bf16),
            pltpu.VMEM((steps, tps, q, width), bf16),
            pltpu.VMEM((steps, tps, q, width), bf16),
            pltpu.VMEM((steps, q, width), bf16),
            pltpu.VMEM((steps, reps, q, rank), bf16),
            pltpu.VMEM((steps, reps, q, rank), bf16),
            pltpu.VMEM((steps, reps, q, rank), bf16),
            pltpu.VMEM((steps, tps, q, rank), bf16),
            pltpu.VMEM((reps * q, out_share * rank), bf16),
            dma((3,)),
            dma((steps,)),
            dma((steps,)),
            dma((steps, reps)),
            dma((steps, reps)),
            dma((steps, reps)),
            dma((steps, reps)),
            dma((steps, reps)),
            dma((steps, tps)),
            dma((steps, tps)),
            dma((steps, reps)),
            dma((steps, reps)),
            dma((steps, tps)),
            dma((steps, tps)),
            dma((steps, tps)),
            dma((steps, tps)),
        ],
        compiler_params=pltpu.CompilerParams(
            collective_id=0, has_side_effects=True, vmem_limit_bytes=48 << 20
        ),
    )(tokens, weight, factors_in, factors_out, by_step(adapter), by_step(scale))


def solution(mesh):
    placed = (
        P(("parts", "rep"), "tp"),
        P("tp", "rep"),
        P("parts"),
        P(),
        P("rep", "tp", None),
        P("tp", None, "rep"),
    )
    return jax.shard_map(
        functools.partial(body, mesh.shape["rep"], mesh.shape["tp"]),
        mesh=mesh,
        in_specs=placed,
        out_specs=P(("parts", "tp"), "rep"),
        check_vma=False,
    )
```

time: 232 us -> 151 us (0.65)
  waiting for transfers between devices: 191 us -> 0 us
  Pallas kernels: 0 us -> 144 us
  matrix products: 24.5 us -> 0 us
  between operations: 13.2 us -> 0.06 us
  local copies, waits for them, and re-layouts: 0.01 us -> 5.69 us
    pallas_call x0 -> x1, Pallas kernels: none -> 144 us  [body(): pl.pallas_call(functools.partial(kernel, reps, tps, steps), out_shape=jax...]
    reduce_scatter x1 -> x0, waiting for transfers between devices: 77.4 us -> none  [body(): lax.psum_scatter((base_part + jnp.einsum('zpe,peg->zg', spread_rows, adap...]
    psum x1 -> x0, waiting for transfers between devices: 75.8 us -> none  [body(): lowrank = lax.psum(partial_value, ('rep', 'tp'))]
    all_gather x1 -> x0, waiting for transfers between devices: 37.3 us -> none  [body(): collected_factors = lax.all_gather(tokens, 'rep', axis=0, tiled=True)]
    dot_general x3 -> x0, matrix products: 24.5 us -> none  [the longest x1 14.4 us: body(): jnp.dot(collected_factors, base_output_weight, preferred_element_type=jnp...]
    unnamed x2 -> x7, local copies, waits for them, and re-layouts: 0.01 us -> 4.64 us
  transfers between devices with their start and end apart: 3 -> 0, of which waited for: 3 -> 0; matrix products, arithmetic and copies ran while one was open for 7% -> 0% of each run, Pallas kernels for 0% -> 0%
where the time goes in v1:
time: 151 us
  Pallas kernels  144 us (95%)
  local copies, waits for them, and re-layouts  5.69 us (4%)
    pallas_call x1, Pallas kernels, body(): pl.pallas_call(functools.partial(kernel, reps, tps, steps), out_shape=jax...  144 us
    unnamed x7, local copies, waits for them, and re-layouts  4.64 us

profile of v1, /device:TPU:0, one launch (start us, length us, event | category | flops | bytes accessed | tf_op | source)
XLA Modules:
  0.0 150.8 jit_solution(2984381061032138578)
XLA Ops:
  0.0 0.8 select_reduce_fusion
  0.8 0.1 mul.18
  0.9 0.8 broadcast_in_dim.40
  1.7 0.3 fusion.scale
  2.0 0.2 broadcast_bitcast_fusion.adapter
  2.2 0.0 copy-start
  2.2 1.2 copy-done
  3.4 0.0 copy-start.1
  3.4 1.2 copy-done.1
  4.7 0.0 copy-start.2
  4.7 1.2 copy-done.2
  5.9 143.9 %shard_map.64 = bf16[256,2048]{1,0:T(8,128)(2,1)S(1)} custom-call(bf16[256,2048]{1,0:T(8,128)(2,1)S(1)} %copy-done, bf16[2048,2048]{1,0:T(8,128)(2,1)} %weight.1, bf16[2,2048,128]{2,1,0:T(8,128)(2,1)S(1)} %copy-done.1, bf16[2,128,2048]{2,1,0:T(8,128)(2,1)S(1)} %copy-done.2, s32[4,4,64,128]{3,2,1,0:T(8,128)S(1)} %broadcast_bitcast_fusion.adapter, ...), custom_call_target="tpu_custom_call" | custom-call | tf_op jit(solution)/shard_map/pallas_call | solution.py:314
  149.8 1.0 copy.14
  (5 shorter events, 0.0 us)
Async XLA Ops:
  2.2 1.2 copy-start
  3.4 1.2 copy-start.1
  4.7 1.2 copy-start.2

commit v2 on v1

--- a/solution.py
+++ b/solution.py
@@ -8,7 +8,8 @@
 from jax.sharding import PartitionSpec as P
 
 RBLK = 16
-STEPS = 4
+STEPS = 8
+AHEAD = 2
 MESH = pl.DeviceIdType.MESH
 
 
@@ -188,85 +189,109 @@
     above = jnp.minimum(t + 1, tps - 1)
     below = jnp.maximum(t - 1, 0)
 
-    def ends_send(s):
+    def ends_send(s, first, end):
         @pl.when(t == 0)
         def _():
-            for b in range(tps - 1, 0, -1):
-                up_copy(s, acc, b, 1).start()
+            for k in range(first, end):
+                up_copy(s, acc, tps - 1 - k, 1).start()
 
         @pl.when(t == tps - 1)
         def _():
-            for b in range(tps - 1):
-                down_copy(s, acc, b, tps - 2).start()
+            for k in range(first, end):
+                down_copy(s, acc, k, tps - 2).start()
 
     def write(s):
-        return pltpu.make_async_copy(done.at[s], out.at[pl.ds(s * q, q)], out_sem.at[s])
-
-    def pass_on(s):
-        for j in range(tps):
+        return pltpu.make_async_copy(done.at[s], out.at[pl.ds(pl.multiple_of(s * q, q), q)], out_sem.at[s])
+
+    far = jnp.maximum(t, tps - 1 - t)
+
+    def pass_on(slot):
+        s_up, s_down, s_end = slot - t, slot - (tps - 1 - t), slot - far
+        ups = (t > 0) & (s_up >= 0) & (s_up < steps)
+        downs = (t < tps - 1) & (s_down >= 0) & (s_down < steps)
+
+        @pl.loop(0, tps)
+        def _(j):
             b = tps - 1 - j
 
-            @pl.when((t > 0) & (b > t))
+            @pl.when(ups & (b > t))
             def _():
-                up_copy(s, up, b, t - 1).wait_recv()
-                up[s, b] = (up[s, b].astype(f32) + acc[s, b].astype(f32)).astype(bf16)
-                up_copy(s, up, b, t + 1).start()
-
-            @pl.when((t < tps - 1) & (j < t))
+                up_copy(s_up, up, b, below).wait_recv()
+                up[s_up, b] = (up[s_up, b].astype(f32) + acc[s_up, b].astype(f32)).astype(bf16)
+                up_copy(s_up, up, b, above).start()
+
+            @pl.when(downs & (j < t))
             def _():
-                down_copy(s, down, j, t + 1).wait_recv()
-                down[s, j] = (down[s, j].astype(f32) + acc[s, j].astype(f32)).astype(bf16)
-                down_copy(s, down, j, t - 1).start()
-
-        @pl.when(t == 0)
-        def _():
-            down_copy(s, down, 0, 1).wait_recv()
-            done[s] = (acc[s, 0].astype(f32) + down[s, 0].astype(f32)).astype(bf16)
-
-        @pl.when(t == tps - 1)
-        def _():
-            up_copy(s, up, tps - 1, tps - 2).wait_recv()
-            done[s] = (acc[s, tps - 1].astype(f32) + up[s, tps - 1].astype(f32)).astype(bf16)
-
-        @pl.when((t > 0) & (t < tps - 1))
-        def _():
-            up_copy(s, up, t, t - 1).wait_recv()
-            down_copy(s, down, t, t + 1).wait_recv()
-            done[s] = (
-                acc[s, t].astype(f32) + up[s, t].astype(f32) + down[s, t].astype(f32)
+                down_copy(s_down, down, j, above).wait_recv()
+                down[s_down, j] = (
+                    down[s_down, j].astype(f32) + acc[s_down, j].astype(f32)
+                ).astype(bf16)
+                down_copy(s_down, down, j, below).start()
+
+        ended = (s_end >= 0) & (s_end < steps)
+
+        @pl.when(ended & (t == 0))
+        def _():
+            down_copy(s_end, down, 0, 1).wait_recv()
+            done[s_end] = (acc[s_end, 0].astype(f32) + down[s_end, 0].astype(f32)).astype(bf16)
+
+        @pl.when(ended & (t == tps - 1))
+        def _():
+            up_copy(s_end, up, tps - 1, tps - 2).wait_recv()
+            done[s_end] = (
+                acc[s_end, tps - 1].astype(f32) + up[s_end, tps - 1].astype(f32)
             ).astype(bf16)
 
-        write(s).start()
-
-    gather_start(0)
+        @pl.when(ended & (t > 0) & (t < tps - 1))
+        def _():
+            up_copy(s_end, up, t, t - 1).wait_recv()
+            down_copy(s_end, down, t, t + 1).wait_recv()
+            done[s_end] = (
+                acc[s_end, t].astype(f32) + up[s_end, t].astype(f32) + down[s_end, t].astype(f32)
+            ).astype(bf16)
+
+        @pl.when(ended)
+        def _():
+            write(s_end).start()
+
+    def rows_in(s):
+        if s < steps:
+            gather_finish(s)
+            if s + AHEAD < steps:
+                gather_start(s + AHEAD)
+            lowrank_ask(s)
+
+    for s in range(min(AHEAD, steps)):
+        gather_start(s)
     loads[0].wait()
-    gather_finish(0)
+    rows_in(0)
+    rows_in(1)
+    lowrank_sum(0)
+    rows_in(2)
+    lowrank_scale(0)
     if steps > 1:
-        gather_start(1)
-    lowrank_ask(0)
+        lowrank_sum(1)
     loads[1].wait()
     project(0)
-    lowrank_sum(0)
-    lowrank_scale(0)
     loads[2].wait()
     for s in range(steps):
-        more = s + 1 < steps
-        if more:
-            gather_finish(s + 1)
-            if s + 2 < steps:
-                gather_start(s + 2)
-            lowrank_ask(s + 1)
         lowrank_wait(s)
         adapt(s)
-        if more:
-            lowrank_sum(s + 1)
-        ends_send(s)
-        if more:
+        ends_send(s, 0, 1)
+        if s + 2 < steps:
+            lowrank_sum(s + 2)
+        ends_send(s, 1, tps - 1)
+        if s + 1 < steps:
+            lowrank_scale(s + 1)
+        rows_in(s + 3)
+        if s + 1 < steps:
             project(s + 1)
-            lowrank_scale(s + 1)
         if s > 0:
-            pass_on(s - 1)
-    pass_on(steps - 1)
+            pass_on(s)
+
+    @pl.loop(steps, steps + tps - 1)
+    def _(slot):
+        pass_on(slot)
 
     for s in range(steps):
         for j, peer in enumerate(peers):

time: 151 us -> 113 us (0.75)
  Pallas kernels: 144 us -> 105 us
    pallas_call x1, Pallas kernels: 144 us -> 105 us  [body(): pl.pallas_call(functools.partial(kernel, reps, tps, steps), out_shape=jax...]
where the time goes in v2:
time: 113 us; the launch traced here: 112 us
  Pallas kernels  105 us (93%)
  local copies, waits for them, and re-layouts  5.68 us (5%)
    pallas_call x1, Pallas kernels, body(): pl.pallas_call(functools.partial(kernel, reps, tps, steps), out_shape=jax...  105 us
    unnamed x7, local copies, waits for them, and re-layouts  4.64 us

profile of v2, /device:TPU:0, one launch (start us, length us, event | category | flops | bytes accessed | tf_op | source)
XLA Modules:
  0.0 112.3 jit_solution(17288102260072265709)
XLA Ops:
  0.0 0.8 select_reduce_fusion
  0.8 0.1 mul.18
  0.9 0.8 broadcast_in_dim.40
  1.7 0.3 fusion.scale
  2.0 0.2 broadcast_bitcast_fusion.adapter
  2.2 0.0 copy-start
  2.2 1.2 %copy-done = bf16[256,2048]{1,0:T(8,128)(2,1)S(1)} copy-done((bf16[256,2048]{1,0:T(8,128)(2,1)S(1)}, bf16[256,2048]{1,0:T(8,128)(2,1)}, u32[]{:S(2)}) %copy-start) | copy-done | bytes 1048600
  3.4 0.0 copy-start.1
  3.4 1.2 %copy-done.1 = bf16[2,2048,128]{2,1,0:T(8,128)(2,1)S(1)} copy-done((bf16[2,2048,128]{2,1,0:T(8,128)(2,1)S(1)}, bf16[2,2048,128]{2,1,0:T(8,128)(2,1)}, u32[]{:S(2)}) %copy-start.1) | copy-done | bytes 1048600
  4.7 0.0 copy-start.2
  4.7 1.2 %copy-done.2 = bf16[2,128,2048]{2,1,0:T(8,128)(2,1)S(1)} copy-done((bf16[2,128,2048]{2,1,0:T(8,128)(2,1)S(1)}, bf16[2,128,2048]{2,1,0:T(8,128)(2,1)}, u32[]{:S(2)}) %copy-start.2) | copy-done | bytes 1048600
  5.9 105.4 %shard_map.64 = bf16[256,2048]{1,0:T(8,128)(2,1)S(1)} custom-call(bf16[256,2048]{1,0:T(8,128)(2,1)S(1)} %copy-done, bf16[2048,2048]{1,0:T(8,128)(2,1)} %weight.1, bf16[2,2048,128]{2,1,0:T(8,128)(2,1)S(1)} %copy-done.1, bf16[2,128,2048]{2,1,0:T(8,128)(2,1)S(1)} %copy-done.2, s32[8,4,32,128]{3,2,1,0:T(8,128)S(1)} %broadcast_bitcast_fusion.adapter, ...), custom_call_target="tpu_custom_call" | custom-call | tf_op jit(solution)/shard_map/pallas_call | solution.py:339
  111.3 1.0 copy.14
  (5 shorter events, 0.0 us)
Async XLA Ops:
  2.2 1.2 %copy-start = (bf16[256,2048]{1,0:T(8,128)(2,1)S(1)}, bf16[256,2048]{1,0:T(8,128)(2,1)}, u32[]{:S(2)}) copy-start(bf16[256,2048]{1,0:T(8,128)(2,1)} %tokens.1) | copy-start | bytes 3145732
  3.4 1.2 %copy-start.1 = (bf16[2,2048,128]{2,1,0:T(8,128)(2,1)S(1)}, bf16[2,2048,128]{2,1,0:T(8,128)(2,1)}, u32[]{:S(2)}) copy-start(bf16[2,2048,128]{2,1,0:T(8,128)(2,1)} %factors_in.1) | copy-start | bytes 3145732
  4.7 1.2 %copy-start.2 = (bf16[2,128,2048]{2,1,0:T(8,128)(2,1)S(1)}, bf16[2,128,2048]{2,1,0:T(8,128)(2,1)}, u32[]{:S(2)}) copy-start(bf16[2,128,2048]{2,1,0:T(8,128)(2,1)} %factors_out.1) | copy-start | bytes 3145732

commit v3 on v2

--- a/solution.py
+++ b/solution.py
@@ -267,12 +267,12 @@
     rows_in(0)
     rows_in(1)
     lowrank_sum(0)
-    rows_in(2)
+    loads[1].wait()
+    project(0)
     lowrank_scale(0)
     if steps > 1:
         lowrank_sum(1)
-    loads[1].wait()
-    project(0)
+    rows_in(2)
     loads[2].wait()
     for s in range(steps):
         lowrank_wait(s)
@@ -374,7 +374,7 @@
             dma((steps, tps)),
         ],
         compiler_params=pltpu.CompilerParams(
-            collective_id=0, has_side_effects=True, vmem_limit_bytes=48 << 20
+            collective_id=0, has_side_effects=True, vmem_limit_bytes=63 << 20
         ),
     )(tokens, weight, factors_in, factors_out, by_step(adapter), by_step(scale))
 

time: 113 us -> 112 us (level)
  local copies, waits for them, and re-layouts: 5.68 us -> 4.15 us
    unnamed x7 -> x1, local copies, waits for them, and re-layouts: 4.64 us -> 2.3 us
where the time goes in v3:
time: 112 us
  Pallas kernels  105 us (94%)
  local copies, waits for them, and re-layouts  4.15 us (4%)
  other arithmetic  1.95 us (2%)
    pallas_call x1, Pallas kernels, body(): pl.pallas_call(functools.partial(kernel, reps, tps, steps), out_shape=jax...  105 us
    unnamed x1, local copies, waits for them, and re-layouts  2.3 us

profile of v3, /device:TPU:0, one launch (start us, length us, event | category | flops | bytes accessed | tf_op | source)
XLA Modules:
  0.0 111.6 jit_solution(14235066365235213641)
XLA Ops:
  0.0 0.8 select_reduce_fusion
  0.8 0.1 mul.18
  0.9 0.8 broadcast_in_dim.40
  1.7 1.2 %fusion.scale = f32[8,4,32,128]{3,2,1,0:T(8,128)} fusion(f32[8,4,32]{2,1,0:T(4,128)S(1)} %copy.12, s32[8,4,32]{2,1,0:T(4,128)S(1)} %copy.11), kind=kLoop, calls=%fused_computation.1 | loop fusion | flops 262144 | bytes 532480 | tf_op jit(solution)/shard_map/jit(_where)/select_n | solution.py:329
  2.8 1.0 broadcast_bitcast_fusion.adapter
  3.8 105.5 %shard_map.64 = bf16[256,2048]{1,0:T(8,128)(2,1)} custom-call(bf16[256,2048]{1,0:T(8,128)(2,1)} %tokens.1, bf16[2048,2048]{1,0:T(8,128)(2,1)} %weight.1, bf16[2,2048,128]{2,1,0:T(8,128)(2,1)} %factors_in.1, bf16[2,128,2048]{2,1,0:T(8,128)(2,1)} %factors_out.1, s32[8,4,32,128]{3,2,1,0:T(8,128)} %broadcast_bitcast_fusion.adapter, f32[8,4,32,128]{3,2,1,0:T(8,128)} %fusion.scale), custom_call_target="tpu_custom_call" | custom-call | tf_op jit(solution)/shard_map/pallas_call | solution.py:339
  109.3 2.3 %copy.14 = bf16[256,2048]{1,0:T(8,128)(2,1)} copy(bf16[256,2048]{1,0:T(8,128)(2,1)} %shard_map.64) | data formatting | bytes 2097152
  (5 shorter events, 0.0 us)
